TPU v7x, 32 devices: a whole 2x2x4 slice. The times are simulated.
32 devices in a mesh: genome: 16 (over z, y, x), heads: 2 (over core).
Axes of the slice: x: 2, y: 2, z: 4, core: 2. Of those that a mesh axis runs over, the one named last changes fastest.
Arguments:
- features_in: bfloat16 [1536, 16384], P('heads', 'genome'), may hold values from -6 to 6
- norm_scale: float32 [2, 1536], P(None, 'heads'), may hold values from 0.5 to 2
- norm_shift: float32 [2, 1536], P(None, 'heads'), may hold values from -3 to 3
- conv_weight: bfloat16 [2, 3, 1536, 1536], P(None, None, 'heads'), may hold values from -0.09375 to 0.09375
- head_weight: bfloat16 [1536, 4096], P('heads'), may hold values from -0.15625 to 0.15625
- assay_head_lists: int32 [16, 4], P('genome'), may hold values from 0 to 31, as said below
- assay_list_counts: int32 [16], P('genome'), may hold values from 1 to 4, as said below
- targets: bfloat16 [16384, 4, 128], P('genome'), may hold values from 0 to 3
Outputs:
- features: bfloat16 [1536, 16384], P('heads', 'genome')
- head_grad: float32 [4096, 1536], P('genome', 'heads')
Inputs may be any that keep to these rules, and one draw needn't show every extreme that they name: Slots at or past assay_list_counts of a bin block hold ids that are unused. Some bin block uses all 4 slots. `assay_head_lists`: the ids within one row are distinct.
All inputs are finite; a program needn't handle non-finite values.
Results may differ from a plain program's by a relative error of at most 0.0085.
Values may be sent and summed in bfloat16 or wider, within the bound.
A program may use at most 128 MiB of HBM per device.

v0:
```python
import jax
import jax.numpy as jnp
from jax import lax
from jax.sharding import PartitionSpec as P

BLOCK = 128
TYPES = 4096
LIST = 4
LAYERS = 2
BASE_DILATION = 4
BIN_DEV = 1024
HEAD_BLOCK_COUNT = 32


def extended(cells, sides, width):
    for axis, dim in sides:
        count = lax.axis_size(axis)
        ends = count - 1
        head = lax.slice_in_dim(cells, 0, width, axis=dim)
        tail = lax.slice_in_dim(cells, cells.shape[dim] - width, cells.shape[dim], axis=dim)
        cells = jnp.concatenate(
            [
                lax.ppermute(tail, axis, [(i, (i + 1) % count) for i in range(ends)]),
                cells,
                lax.ppermute(head, axis, [((i + 1) % count, i) for i in range(ends)]),
            ],
            axis=dim,
        )
    return cells


def on_device(
    features_in,
    norm_scale,
    norm_shift,
    conv_weight,
    head_weight,
    assay_head_lists,
    assay_list_counts,
    targets,
):
    share_cols = features_in.shape[0]
    rows = features_in.shape[1]
    x = features_in
    for layer_index in range(LAYERS):
        dilation_step = BASE_DILATION * 2**layer_index
        taps = conv_weight[layer_index]
        u = jax.nn.gelu(
            x.astype(jnp.float32) * norm_scale[layer_index][:, None]
            + norm_shift[layer_index][:, None],
            approximate=False,
        ).astype(jnp.bfloat16)
        padded_input = extended(u, (("genome", 1),), dilation_step)

        def add_taps(total, piece, start, taps=taps, dilation_step=dilation_step):
            for k in range(3):
                part_w = taps[k]
                total = total + jnp.dot(
                    part_w,
                    piece[:, k * dilation_step : k * dilation_step + rows],
                    preferred_element_type=jnp.float32,
                )
            return total

        empty = jnp.zeros((share_cols, rows), jnp.float32)
        branch = add_taps(
            empty, lax.all_gather(padded_input, "heads", axis=0, tiled=True), jnp.int32(0)
        )
        x = (x.astype(jnp.float32) + branch).astype(jnp.bfloat16)
    ids = assay_head_lists[0]
    count = assay_list_counts[0]
    blocks = head_weight.reshape(share_cols, HEAD_BLOCK_COUNT, BLOCK)
    chosen = blocks[:, ids]
    active = (jnp.arange(LIST, dtype=jnp.int32) < count).astype(jnp.float32)
    partial_z = jnp.einsum("ci,cst->ist", x, chosen, preferred_element_type=jnp.float32)
    z = lax.psum(partial_z, "heads")
    slope = (
        (jax.nn.softplus(z) - targets.astype(jnp.float32))
        * jax.nn.sigmoid(z)
        * active[None, :, None]
        / BIN_DEV
    ).astype(jnp.bfloat16)
    term = jnp.einsum("ist,ci->stc", slope, x, preferred_element_type=jnp.float32)
    onehot = (ids[None, :] == jnp.arange(HEAD_BLOCK_COUNT, dtype=jnp.int32)[:, None]).astype(
        jnp.float32
    )
    dense = jnp.einsum("bs,stc->btc", onehot, term).reshape(TYPES, share_cols)
    head_grad = lax.psum_scatter(dense, "genome", scatter_dimension=0, tiled=True)
    return (x, head_grad)


def solution(mesh):
    return jax.shard_map(
        on_device,
        mesh=mesh,
        in_specs=(
            P("heads", "genome"),
            P(None, "heads"),
            P(None, "heads"),
            P(None, None, "heads", None),
            P("heads", None),
            P("genome", None),
            P("genome"),
            P("genome", None, None),
        ),
        out_specs=(P("heads", "genome"), P("genome", "heads")),
        check_vma=False,
    )
```

profile of v0, /device:TPU:0, one launch (start us, length us, event | category | flops | bytes accessed | tf_op | source)
XLA Modules:
  0.0 382.2 jit_solution(2233192779957629980)
XLA Ops:
  7.2 0.0 copy-start
  7.2 0.0 copy-start.1
  7.2 0.0 all-gather.3.cloned.1.call-start
  7.2 1.7 copy.17
  9.0 0.0 copy-done
  9.0 0.0 copy-done.1
  9.0 7.2 %fusion.4 = bf16[768,1024]{0,1:T(8,128)(2,1)S(1)} fusion(bf16[768,1024]{0,1:T(8,128)(2,1)S(1)} %copy.17, f32[768]{0:T(1024)S(1)} %get-tuple-element.11, f32[768]{0:T(1024)S(1)} %get-tuple-element.18), kind=kLoop, calls=%fused_computation.12 | loop fusion | flops 53477376 | bytes 3151872 | tf_op jit(solution)/shard_map/convert_element_type | solution.py:52
  16.2 1.3 collective-permute-start.1
  17.5 5.5 %collective-permute-start = (bf16[768,4]{0,1:T(4,128)(2,1)S(1)}, bf16[768,4]{0,1:T(4,128)(2,1)S(1)}, u32[]{:S(2)}, u32[]{:S(2)}) collective-permute-start(bf16[768,4]{0,1:T(4,128)(2,1)S(1)} %get-tuple-element.15), channel_id=1, source_target_pairs={{0,2},{2,4},{4,6},{6,8},{8,10},{10,12},{12,14},{14,16},{16,18},{18... | collective-permute-start | bytes 18440 | tf_op jit(solution)/shard_map/ppermute | solution.py:23
  23.0 0.0 collective-permute-done.1
  23.0 1.3 collective-permute-done
  24.3 9.1 %concatenate.6 = bf16[768,1032]{0,1:T(8,128)(2,1)} concatenate(bf16[768,4]{0,1:T(4,128)(2,1)S(1)} %collective-permute-done, bf16[768,1024]{0,1:T(8,128)(2,1)S(1)} %fusion.4, bf16[768,4]{0,1:T(4,128)(2,1)S(1)} %collective-permute-done.1), dimensions={1} | concatenate | bytes 3170304 | tf_op jit(solution)/shard_map/concatenate | solution.py:21
  33.4 0.0 all-gather.3.cloned.1.call-update
  33.5 0.0 all-gather.5.cloned.1.call-start
  33.5 16.5 %all-gather.3.cloned.1.call-done = bf16[1536,1032]{0,1:T(8,128)(2,1)} async-done(((bf16[768,1032]{0,1:T(8,128)(2,1)}), bf16[1536,1032]{0,1:T(8,128)(2,1)}) %all-gather.3.cloned.1.call-update) | async-done | bytes 3170320 | tf_op jit(solution)/shard_map/all_gather | solution.py:67
  50.0 5.4 %fusion.34 = f32[1024,768]{1,0:T(8,128)S(1)} fusion(bf16[1536,1032]{0,1:T(8,128)(2,1)} %all-gather.3.cloned.1.call-done, bf16[2,3,768,1536]{3,2,1,0:T(8,128)(2,1)} %param.11), kind=kOutput, calls=%fused_computation.42 | convolution fusion | flops 2415919104 | bytes 8650752 | tf_op jit(solution)/shard_map/dot_general | solution.py:58
  55.5 0.0 copy-done.4
  55.5 4.3 %fusion.36 = f32[1024,768]{1,0:T(8,128)S(1)} fusion(bf16[1536,1032]{0,1:T(8,128)(2,1)S(1)} %copy-done.4, bf16[2,3,768,1536]{3,2,1,0:T(8,128)(2,1)} %param.11), kind=kOutput, calls=%fused_computation.44 | convolution fusion | flops 2415919104 | bytes 8650752 | tf_op jit(solution)/shard_map/dot_general | solution.py:58
  59.8 13.0 %fusion.17 = (bf16[768,1024]{0,1:T(8,128)(2,1)S(1)}, bf16[768,1024]{0,1:T(8,128)(2,1)}) fusion(f32[768]{0:T(1024)S(1)} %get-tuple-element.10, f32[768]{0:T(1024)S(1)} %get-tuple-element.19, bf16[2,3,768,1536]{3,2,1,0:T(8,128)(2,1)} %param.11, bf16[1536,1032]{0,1:T(8,128)(2,1)S(1)} %copy-done.4, f32[1024,768]{1,0:T(8,128)S(1)} %fusion.36, ...), kind=kOutput, calls=%fused_computation.25 | convolution fusion | flops 2473328640 | bytes 16523264 | tf_op jit(solution)/shard_map/dot_general | solution.py:58
  72.8 3.6 collective-permute-start.2
  76.5 1.3 collective-permute-start.3
  77.8 0.1 collective-permute-done.2
  77.8 4.2 %collective-permute-done.3 = bf16[768,8]{0,1:T(8,128)(2,1)S(1)} collective-permute-done((bf16[768,8]{0,1:T(8,128)(2,1)S(1)}, bf16[768,8]{0,1:T(8,128)(2,1)S(1)}, u32[]{:S(2)}, u32[]{:S(2)}) %collective-permute-start.3) | collective-permute-done | bytes 12320 | tf_op jit(solution)/shard_map/ppermute | solution.py:25
  82.0 1.2 pad_maximum_fusion
  83.3 0.0 all-gather.5.cloned.1.call-update
  83.3 0.2 all-reduce.2.cloned.1.call-start
  83.5 8.6 %copy.18 = bf16[768,4096]{0,1:T(8,128)(2,1)} copy(bf16[768,4096]{1,0:T(8,128)(2,1)} %param.12) | data formatting | bytes 12582912 | tf_op args[4]
  92.2 8.7 %copy.19 = bf16[768,32,128]{2,0,1:T(8,128)(2,1)} copy(bf16[768,32,128]{0,2,1:T(8,128)(2,1)} %bitcast.50) | data formatting | bytes 12582912 | tf_op jit(solution)/shard_map/reshape | solution.py:72
  100.9 0.0 copy-done.2
  100.9 3.5 gather_fusion
  104.4 0.0 all-gather.5.cloned.1.call-done
  104.4 0.0 copy-start.3
  104.4 5.4 %fusion.28 = f32[1024,768]{1,0:T(8,128)S(1)} fusion(bf16[1536,1040]{0,1:T(8,128)(2,1)} %all-gather.5.cloned.1.call-done, bf16[2,3,768,1536]{3,2,1,0:T(8,128)(2,1)} %param.11), kind=kOutput, calls=%fused_computation.36 | convolution fusion | flops 2415919104 | bytes 8650752 | tf_op jit(solution)/shard_map/dot_general | solution.py:58
  109.8 0.0 copy-done.3
  109.8 0.0 copy-start.6
  109.8 4.4 %fusion.30 = f32[1024,768]{1,0:T(8,128)S(1)} fusion(bf16[1536,1040]{0,1:T(8,128)(2,1)S(1)} %copy-done.3, bf16[2,3,768,1536]{3,2,1,0:T(8,128)(2,1)} %param.11), kind=kOutput, calls=%fused_computation.38 | convolution fusion | flops 2415919104 | bytes 8650752 | tf_op jit(solution)/shard_map/dot_general | solution.py:58
  114.2 4.5 %fusion.25 = bf16[768,1024]{0,1:T(8,128)(2,1)S(1)} fusion(bf16[768,1024]{0,1:T(8,128)(2,1)S(1)} %copy-done.6, f32[1024,768]{1,0:T(8,128)S(1)} %fusion.30, f32[1024,768]{1,0:T(8,128)S(1)} %fusion.28, bf16[2,3,768,1536]{3,2,1,0:T(8,128)(2,1)} %param.11, bf16[1536,1040]{0,1:T(8,128)(2,1)S(1)} %copy-done.3), kind=kOutput, calls=%fused_computation.33 | convolution fusion | flops 2419851264 | bytes 14942208 | tf_op jit(solution)/shard_map/dot_general | solution.py:58
  118.8 0.0 copy-start.5
  118.8 2.3 fusion.79
  121.1 0.0 all-reduce.2.cloned.1.call-update
  121.1 0.0 reduce-scatter.2.cloned.1.call-start
  121.8 22.6 %all-reduce.2.cloned.1.call-done = f32[1024,4,128]{2,0,1:T(8,128)} async-done(((f32[1024,4,128]{2,0,1:T(8,128)}), f32[1024,4,128]{2,0,1:T(8,128)}) %all-reduce.2.cloned.1.call-update) | async-done | bytes 2097168 | tf_op jit(solution)/shard_map/psum | solution.py:76
  144.4 4.0 %fusion.77 = bf16[4,128,768]{2,1,0:T(8,128)(2,1)S(1)} fusion(bf16[768,1024]{0,1:T(8,128)(2,1)S(1)} %fusion.25, f32[1024,4,128]{2,0,1:T(8,128)} %all-reduce.2.cloned.1.call-done, bf16[1024,4,128]{2,1,0:T(4,128)(2,1)S(1)} %copy-done.5, f32[4]{0:T(128)S(1)} %compare_convert_fusion), kind=kOutput, calls=%fused_computation.86 | convolution fusion | flops 813170688 | bytes 5505040 | tf_op jit(solution)/shard_map/ist,ci->stc/dot_general | solution.py:83
  148.5 5.7 %fusion.81 = f32[32,128,768]{2,0,1:T(8,128)} fusion(bf16[4,128,768]{2,1,0:T(8,128)(2,1)S(1)} %fusion.77, s32[4]{0:T(128)S(1)} %bitcast.51), kind=kOutput, calls=%fused_computation.90 | convolution fusion | flops 25165952 | bytes 13369360 | tf_op jit(solution)/shard_map/bs,stc->btc/dot_general | solution.py:87
  154.2 16.3 %copy.24 = f32[32,128,768]{2,1,0:T(8,128)} copy(f32[32,128,768]{2,0,1:T(8,128)} %fusion.81) | data formatting | bytes 25165824 | tf_op jit(solution)/shard_map/bs,stc->btc/dot_general | solution.py:87
  170.5 0.0 reduce-scatter.2.cloned.1.call-update
  170.5 1.6 copy.25
  172.1 203.5 %reduce-scatter.2.cloned.1.call-done = f32[256,768]{1,0:T(8,128)} async-done(((f32[4096,768]{1,0:T(8,128)}), f32[256,768]{1,0:T(8,128)}) %reduce-scatter.2.cloned.1.call-update) | async-done | bytes 786448 | tf_op jit(solution)/shard_map/reduce_scatter | solution.py:88
  (10 shorter events, 0.1 us)
Async XLA Ops:
  7.2 1.8 copy-start
  7.2 1.8 copy-start.1
  7.2 42.9 %all-gather.3.cloned.1.call-start = ((), (), s32[]{:S(2)}) async-start(), calls=%async_computation.1 | async-start | bytes 4755456 | tf_op jit(solution)/shard_map/all_gather | solution.py:67
  16.2 6.8 %collective-permute-start.1 = (bf16[768,4]{0,1:T(4,128)(2,1)S(1)}, bf16[768,4]{0,1:T(4,128)(2,1)S(1)}, u32[]{:S(2)}, u32[]{:S(2)}) collective-permute-start(bf16[768,4]{0,1:T(4,128)(2,1)S(1)} %get-tuple-element.14), channel_id=1, source_target_pairs={{2,0},{4,2},{6,4},{8,6},{10,8},{12,10},{14,12},{16,14},{18,16},{20... | collective-permute-start | bytes 18440 | tf_op jit(solution)/shard_map/ppermute | solution.py:25
  17.5 6.8 %collective-permute-start = (bf16[768,4]{0,1:T(4,128)(2,1)S(1)}, bf16[768,4]{0,1:T(4,128)(2,1)S(1)}, u32[]{:S(2)}, u32[]{:S(2)}) collective-permute-start(bf16[768,4]{0,1:T(4,128)(2,1)S(1)} %get-tuple-element.15), channel_id=1, source_target_pairs={{0,2},{2,4},{4,6},{6,8},{8,10},{10,12},{12,14},{14,16},{16,18},{18... | collective-permute-start | bytes 18440 | tf_op jit(solution)/shard_map/ppermute | solution.py:23
  33.5 70.9 %all-gather.5.cloned.1.call-start = ((), (), s32[]{:S(2)}) async-start(), calls=%async_computation.2 | async-start | bytes 4792320 | tf_op jit(solution)/shard_map/all_gather | solution.py:67
  50.0 5.4 %copy-start.4 = (bf16[1536,1032]{0,1:T(8,128)(2,1)S(1)}, bf16[1536,1032]{0,1:T(8,128)(2,1)}, u32[]{:S(2)}) copy-start(bf16[1536,1032]{0,1:T(8,128)(2,1)} %all-gather.3.cloned.1.call-done) | copy-start | bytes 9510916
  72.8 5.0 %collective-permute-start.2 = (bf16[768,8]{0,1:T(8,128)(2,1)S(1)}, bf16[768,8]{0,1:T(8,128)(2,1)S(1)}, u32[]{:S(2)}, u32[]{:S(2)}) collective-permute-start(bf16[768,8]{0,1:T(8,128)(2,1)S(1)} %get-tuple-element.12), channel_id=1, source_target_pairs={{0,2},{2,4},{4,6},{6,8},{8,10},{10,12},{12,14},{14,16},{16,18},{18... | collective-permute-start | bytes 36872 | tf_op jit(solution)/shard_map/ppermute | solution.py:23
  76.5 5.6 %collective-permute-start.3 = (bf16[768,8]{0,1:T(8,128)(2,1)S(1)}, bf16[768,8]{0,1:T(8,128)(2,1)S(1)}, u32[]{:S(2)}, u32[]{:S(2)}) collective-permute-start(bf16[768,8]{0,1:T(8,128)(2,1)S(1)} %get-tuple-element.13), channel_id=1, source_target_pairs={{2,0},{4,2},{6,4},{8,6},{10,8},{12,10},{14,12},{16,14},{18,16},{20... | collective-permute-start | bytes 36872 | tf_op jit(solution)/shard_map/ppermute | solution.py:25
  83.3 61.1 %all-reduce.2.cloned.1.call-start = ((), (), s32[]{:S(2)}) async-start(), calls=%async_computation.3 | async-start | bytes 4194304 | tf_op jit(solution)/shard_map/psum | solution.py:76
  92.2 8.7 %copy-start.2 = (s32[1,4]{1,0:T(1,128)S(1)}, s32[1,4]{1,0:T(1,128)}, u32[]{:S(2)}) copy-start(s32[1,4]{1,0:T(1,128)} %param.13) | copy-start | bytes 52
  104.4 5.4 %copy-start.3 = (bf16[1536,1040]{0,1:T(8,128)(2,1)S(1)}, bf16[1536,1040]{0,1:T(8,128)(2,1)}, u32[]{:S(2)}) copy-start(bf16[1536,1040]{0,1:T(8,128)(2,1)} %all-gather.5.cloned.1.call-done) | copy-start | bytes 9584644
  109.8 4.4 %copy-start.6 = (bf16[768,1024]{0,1:T(8,128)(2,1)S(1)}, bf16[768,1024]{0,1:T(8,128)(2,1)}, u32[]{:S(2)}) copy-start(bf16[768,1024]{0,1:T(8,128)(2,1)} %get-tuple-element.17) | copy-start | bytes 4718596
  118.8 25.7 %copy-start.5 = (bf16[1024,4,128]{2,1,0:T(4,128)(2,1)S(1)}, bf16[1024,4,128]{2,1,0:T(4,128)(2,1)}, u32[]{:S(2)}) copy-start(bf16[1024,4,128]{2,1,0:T(4,128)(2,1)} %param.15) | copy-start | bytes 3145732
  121.1 254.6 %reduce-scatter.2.cloned.1.call-start = ((), (), s32[]{:S(2)}) async-start(), calls=%async_computation.4 | async-start | bytes 13369344 | tf_op jit(solution)/shard_map/reduce_scatter | solution.py:88
Sparse Core Ops, SparseCore 0:
  33.6 16.4 all-gather.2
  83.4 13.9 all-gather.4
  121.2 23.1 all-reduce.1
  170.6 204.9 reduce-scatter.1
where the time goes:
time: 383 us; the launch traced here: 382 us
  waiting for transfers between devices  248 us (65%)
  local copies, waits for them, and re-layouts  49.7 us (13%)
  matrix products  49.1 us (13%)
  between operations  14.6 us (4%)
  starting transfers between devices  12 us (3%)
  other arithmetic  8.43 us (2%)
    reduce_scatter x1, waiting for transfers between devices, on_device(): lax.psum_scatter(dense, 'genome', scatter_dimension=0, tiled=True)  204 us
    dot_general x6, matrix products, add_taps(): jnp.dot(part_w, piece[:, k * dilation_step:k * dilation_step + rows], pre...  37.1 us
    psum x1, waiting for transfers between devices, on_device(): z = lax.psum(partial_z, 'heads')  22.6 us
    all_gather x2, waiting for transfers between devices, on_device(): lax.all_gather(padded_input, 'heads', axis=0, tiled=True)  16.6 us
    dot_general x1, local copies, waits for them, and re-layouts, on_device(): dense = jnp.einsum('bs,stc->btc', onehot, term).reshape(TYPES, share_cols)  16.3 us
    unnamed x17, local copies, waits for them, and re-layouts  12 us
    concatenate x1, local copies, waits for them, and re-layouts, extended(): jnp.concatenate([lax.ppermute(tail, axis, [(i, (i + 1) % count) for i in...  9.1 us
    ppermute x2, starting transfers between devices, extended(): lax.ppermute(tail, axis, [(i, (i + 1) % count) for i in range(ends)])  9.08 us
  transfers between devices with their start and end apart: 8, of which 6 were waited for; matrix products, arithmetic and copies ran while one was open for 6% of the time, Pallas kernels for 0%

commit v1 on v0

--- a/solution.py
+++ b/solution.py
@@ -1,6 +1,10 @@
+import functools
+
 import jax
 import jax.numpy as jnp
 from jax import lax
+from jax.experimental import pallas as pl
+from jax.experimental.pallas import tpu as pltpu
 from jax.sharding import PartitionSpec as P
 
 BLOCK = 128
@@ -10,6 +14,9 @@
 BASE_DILATION = 4
 BIN_DEV = 1024
 HEAD_BLOCK_COUNT = 32
+HALO = 128
+EDGE = 16
+MESH = pl.DeviceIdType.MESH
 
 
 def extended(cells, sides, width):
@@ -29,7 +36,7 @@
     return cells
 
 
-def on_device(
+def on_device_general(
     features_in,
     norm_scale,
     norm_shift,
@@ -51,21 +58,14 @@
             approximate=False,
         ).astype(jnp.bfloat16)
         padded_input = extended(u, (("genome", 1),), dilation_step)
-
-        def add_taps(total, piece, start, taps=taps, dilation_step=dilation_step):
-            for k in range(3):
-                part_w = taps[k]
-                total = total + jnp.dot(
-                    part_w,
-                    piece[:, k * dilation_step : k * dilation_step + rows],
-                    preferred_element_type=jnp.float32,
-                )
-            return total
-
-        empty = jnp.zeros((share_cols, rows), jnp.float32)
-        branch = add_taps(
-            empty, lax.all_gather(padded_input, "heads", axis=0, tiled=True), jnp.int32(0)
-        )
+        piece = lax.all_gather(padded_input, "heads", axis=0, tiled=True)
+        branch = jnp.zeros((share_cols, rows), jnp.float32)
+        for k in range(3):
+            branch = branch + jnp.dot(
+                taps[k],
+                piece[:, k * dilation_step : k * dilation_step + rows],
+                preferred_element_type=jnp.float32,
+            )
         x = (x.astype(jnp.float32) + branch).astype(jnp.bfloat16)
     ids = assay_head_lists[0]
     count = assay_list_counts[0]
@@ -89,9 +89,420 @@
     return (x, head_grad)
 
 
+def gelu(v):
+    return 0.5 * v * (1.0 + lax.erf(v * 0.7071067811865476))
+
+
+def pick_kernel(ids_ref, hw_ref, tg_ref, hw_out, tg_out):
+    hw_out[...] = hw_ref[...].T
+    tg_out[...] = tg_ref[...].T
+
+
+def pick(ids, head_weight, goal):
+    c = head_weight.shape[0]
+    n = goal.shape[0]
+    return pl.pallas_call(
+        pick_kernel,
+        grid_spec=pltpu.PrefetchScalarGridSpec(
+            num_scalar_prefetch=1,
+            grid=(LIST,),
+            in_specs=[
+                pl.BlockSpec((c, BLOCK), lambda s, ids: (0, ids[s])),
+                pl.BlockSpec((n, BLOCK), lambda s, ids: (0, s)),
+            ],
+            out_specs=[
+                pl.BlockSpec((BLOCK, c), lambda s, ids: (s, 0)),
+                pl.BlockSpec((BLOCK, n), lambda s, ids: (s, 0)),
+            ],
+        ),
+        out_shape=[
+            jax.ShapeDtypeStruct((LIST * BLOCK, c), jnp.bfloat16),
+            jax.ShapeDtypeStruct((LIST * BLOCK, n), jnp.bfloat16),
+        ],
+        name="pick",
+    )(ids, head_weight, goal)
+
+
+def trunk_kernel(
+    feat, norm, act, hw, tg, w_hbm,
+    x_out, term,
+    w, xe, u, r, acc, edge_out, edge_in, z_own, z_out, z_in,
+    w_sem, edge_send, edge_recv, u_send, u_recv, z_send, z_recv,
+):
+    c, n = feat.shape
+    wide = n + HALO
+    me = lax.axis_index("genome")
+    h = lax.axis_index("heads")
+    other = 1 - h
+    count = lax.axis_size("genome")
+    right, left = lax.rem(me + 1, count), lax.rem(me + count - 1, count)
+    dot = functools.partial(jnp.dot, preferred_element_type=jnp.float32)
+
+    loads = []
+    for layer in range(LAYERS):
+        for k in range(3):
+            cp = pltpu.make_async_copy(w_hbm.at[layer, k], w.at[layer, k], w_sem.at[layer, k])
+            cp.start()
+            loads.append(cp)
+
+    barrier = pltpu.get_barrier_semaphore()
+    for dev in ((me, other), (left, h), (right, h)):
+        pl.semaphore_signal(barrier, inc=1, device_id=dev, device_id_type=MESH)
+
+    edge_out[0] = feat[:, 0:BLOCK].astype(jnp.float32).T[:EDGE].astype(jnp.bfloat16)
+    edge_out[1] = (
+        feat[:, n - BLOCK : n].astype(jnp.float32).T[BLOCK - EDGE :].astype(jnp.bfloat16)
+    )
+    pl.semaphore_wait(barrier, 3)
+    edges = []
+    for i, dev in enumerate((left, right)):
+        cp = pltpu.make_async_remote_copy(
+            edge_out.at[i], edge_in.at[i], edge_send.at[i], edge_recv.at[i],
+            device_id=(dev, h), device_id_type=MESH,
+        )
+        cp.start()
+        edges.append(cp)
+
+    lane = lax.broadcasted_iota(jnp.int32, (1, wide), 1)
+    inside = jnp.where(
+        lane < n,
+        1.0,
+        jnp.where(
+            lane < n + HALO // 2,
+            jnp.where(me < count - 1, 1.0, 0.0),
+            jnp.where(me > 0, 1.0, 0.0),
+        ),
+    ).astype(jnp.float32)
+
+    pieces = 3
+    step = c // pieces
+
+    def u_copy(layer, m):
+        rows = pl.ds(m * step, step)
+        return pltpu.make_async_remote_copy(
+            u.at[layer, 0, rows], u.at[layer, 1, rows],
+            u_send.at[layer, m], u_recv.at[layer, m],
+            device_id=(me, other), device_id_type=MESH,
+        )
+
+    def shifted(layer, half, rows, val):
+        d = BASE_DILATION * 2**layer
+        r[layer, half, 0, rows, :] = pltpu.roll(val, d, 1).astype(jnp.bfloat16)
+        r[layer, half, 1, rows, :] = pltpu.roll(val, wide - d, 1).astype(jnp.bfloat16)
+
+    def activate(layer, m):
+        @pl.loop(0, step // BLOCK)
+        def _(j):
+            rows = pl.ds(pl.multiple_of(m * step + j * BLOCK, BLOCK), BLOCK)
+            v = xe[layer, rows, :].astype(jnp.float32)
+            a = norm[rows, layer : layer + 1]
+            b = norm[rows, LAYERS + layer : LAYERS + layer + 1]
+            val = (gelu(v * a + b) * inside).astype(jnp.bfloat16)
+            u[layer, 0, rows, :] = val
+            shifted(layer, 0, rows, val.astype(jnp.float32))
+
+    xe[0, :, 0:n] = feat[...]
+    for cp in edges:
+        cp.wait()
+    halo = jnp.concatenate(
+        [
+            edge_in[0].astype(jnp.float32),
+            jnp.zeros((HALO - 2 * EDGE, c), jnp.float32),
+            edge_in[1].astype(jnp.float32),
+        ],
+        axis=0,
+    )
+    xe[0, :, n:wide] = halo.T.astype(jnp.bfloat16)
+
+    def own_part(layer, m, width):
+        rows = pl.ds(pl.multiple_of(m * step, step), step)
+        cols = pl.ds(pl.multiple_of(h * c, c), c)
+        t = dot(w[layer, 0, rows, cols], r[layer, 0, 0, :, 0:width])
+        t = t + dot(w[layer, 1, rows, cols], u[layer, 0, :, 0:width])
+        t = t + dot(w[layer, 2, rows, cols], r[layer, 0, 1, :, 0:width])
+        acc[rows, 0:width] = t
+
+    def other_part(layer, m, width):
+        rows = pl.ds(pl.multiple_of(m * step, step), step)
+        cols = pl.ds(pl.multiple_of(other * c, c), c)
+        t = acc[rows, 0:width] + dot(w[layer, 0, rows, cols], r[layer, 1, 0, :, 0:width])
+        t = t + dot(w[layer, 1, rows, cols], u[layer, 1, :, 0:width])
+        t = t + dot(w[layer, 2, rows, cols], r[layer, 1, 1, :, 0:width])
+        return rows, (xe[layer, rows, 0:width].astype(jnp.float32) + t).astype(jnp.bfloat16)
+
+    copies = []
+    for m in range(pieces):
+        activate(0, m)
+        cp = u_copy(0, m)
+        cp.start()
+        copies.append(cp)
+
+    for layer in range(LAYERS):
+        last = layer == LAYERS - 1
+        width = n if last else wide
+        for k in range(3):
+            loads[3 * layer + k].wait()
+
+        @pl.loop(0, pieces)
+        def _(m, layer=layer, width=width):
+            own_part(layer, m, width)
+
+        for m in range(pieces):
+            copies[m].wait_recv()
+
+            @pl.loop(0, step // BLOCK)
+            def _(j, m=m, layer=layer):
+                rows = pl.ds(pl.multiple_of(m * step + j * BLOCK, BLOCK), BLOCK)
+                shifted(layer, 1, rows, u[layer, 1, rows, :].astype(jnp.float32))
+
+        for m in range(pieces):
+            copies[m].wait_send()
+        copies = []
+        if last:
+
+            @pl.loop(0, pieces)
+            def _(m, layer=layer, width=width):
+                rows, val = other_part(layer, m, width)
+                x_out[rows, :] = val
+        else:
+            for m in range(pieces):
+                rows, val = other_part(layer, m, width)
+                xe[layer + 1, rows, :] = val
+                activate(layer + 1, m)
+                cp = u_copy(layer + 1, m)
+                cp.start()
+                copies.append(cp)
+
+    groups = 2
+    size = LIST * BLOCK // groups
+    sums = []
+    for s in range(groups):
+        rows = pl.ds(s * size, size)
+        part = dot(hw[rows, :], x_out[...])
+        z_own[rows, :] = part
+        z_out[rows, :] = part.astype(jnp.bfloat16)
+        cp = pltpu.make_async_remote_copy(
+            z_out.at[rows], z_in.at[rows], z_send.at[s], z_recv.at[s],
+            device_id=(me, other), device_id_type=MESH,
+        )
+        cp.start()
+        sums.append(cp)
+    for s in range(groups):
+        rows = pl.ds(s * size, size)
+        sums[s].wait()
+        z = z_own[rows, :] + z_in[rows, :].astype(jnp.float32)
+        e = jnp.exp(-jnp.abs(z))
+        soft = jnp.maximum(z, 0.0) + jnp.log1p(e)
+        sig = jnp.where(z >= 0.0, 1.0, e) / (1.0 + e)
+        slope = (
+            (soft - tg[rows, :].astype(jnp.float32)) * sig * (act[rows, :] / BIN_DEV)
+        ).astype(jnp.bfloat16)
+        term[rows, :] = lax.dot_general(
+            slope, x_out[...], (((1,), (1,)), ((), ())), preferred_element_type=jnp.float32
+        ).astype(jnp.bfloat16)
+
+
+def trunk(feat, norm, act, hw, tg, w):
+    c, n = feat.shape
+    wide = n + HALO
+    vmem = pl.BlockSpec(memory_space=pltpu.VMEM)
+    bf16, f32 = jnp.bfloat16, jnp.float32
+    return pl.pallas_call(
+        trunk_kernel,
+        out_shape=[
+            jax.ShapeDtypeStruct((c, n), bf16),
+            jax.ShapeDtypeStruct((LIST * BLOCK, c), bf16),
+        ],
+        in_specs=[vmem] * 5 + [pl.BlockSpec(memory_space=pl.ANY)],
+        out_specs=[vmem, vmem],
+        scratch_shapes=[
+            pltpu.VMEM(w.shape, bf16),
+            pltpu.VMEM((LAYERS, c, wide), bf16),
+            pltpu.VMEM((LAYERS, 2, c, wide), bf16),
+            pltpu.VMEM((LAYERS, 2, 2, c, wide), bf16),
+            pltpu.VMEM((c, wide), f32),
+            pltpu.VMEM((2, EDGE, c), bf16),
+            pltpu.VMEM((2, EDGE, c), bf16),
+            pltpu.VMEM((LIST * BLOCK, n), f32),
+            pltpu.VMEM((LIST * BLOCK, n), bf16),
+            pltpu.VMEM((LIST * BLOCK, n), bf16),
+            pltpu.SemaphoreType.DMA((LAYERS, 3)),
+            pltpu.SemaphoreType.DMA((2,)),
+            pltpu.SemaphoreType.DMA((2,)),
+            pltpu.SemaphoreType.DMA((LAYERS, 3)),
+            pltpu.SemaphoreType.DMA((LAYERS, 3)),
+            pltpu.SemaphoreType.DMA((2,)),
+            pltpu.SemaphoreType.DMA((2,)),
+        ],
+        compiler_params=pltpu.CompilerParams(
+            collective_id=0, has_side_effects=True, vmem_limit_bytes=60 * 2**20
+        ),
+        cost_estimate=pl.CostEstimate(
+            flops=17 * 10**9, bytes_accessed=20 * 2**20, transcendentals=0
+        ),
+        name="trunk",
+    )(feat, norm, act, hw, tg, w)
+
+
+def scatter_kernel(
+    chunks, table, term, out,
+    mine, send2, keep, recv2, send3, recv3,
+    s1, r1, s2, r2, s3, r3,
+    *theirs,
+):
+    me = lax.axis_index("genome")
+    h = lax.axis_index("heads")
+    x, y, z = lax.rem(me, 2), lax.rem(me // 2, 2), me // 4
+    depth = lax.axis_size("genome") // 4
+    across_x = (z * 2 + y) * 2 + (1 - x)
+    across_y = (z * 2 + (1 - y)) * 2 + x
+    part = mine.shape[-1]
+
+    barrier = pltpu.get_barrier_semaphore()
+    peers = [lax.rem(z + i, depth) * 4 + y * 2 + x for i in range(1, depth)]
+    for dev in [across_x, across_y] + peers:
+        pl.semaphore_signal(barrier, inc=1, device_id=(dev, h), device_id_type=MESH)
+    for p in range(chunks):
+        for s in range(LIST):
+            mine[p, s] = term[s * BLOCK : (s + 1) * BLOCK, p * part : (p + 1) * part]
+        mine[p, LIST] = jnp.zeros((BLOCK, part), jnp.bfloat16)
+        theirs[p][LIST] = jnp.zeros((BLOCK, part), jnp.bfloat16)
+    pl.semaphore_wait(barrier, 2 + len(peers))
+
+    first = []
+    for p in range(chunks):
+        cp = pltpu.make_async_remote_copy(
+            mine.at[p, pl.ds(0, LIST)], theirs[p].at[pl.ds(0, LIST)], s1.at[p], r1.at[p],
+            device_id=(across_x if p % 2 == 0 else across_y, h), device_id_type=MESH,
+        )
+        cp.start()
+        first.append(cp)
+    second = []
+    for p in range(chunks):
+        first[p].wait()
+        o = p % 2
+
+        @pl.loop(0, 2 * depth)
+        def _(j, p=p, o=o):
+            a = mine[p, table[o * 32 + j]].astype(jnp.float32)
+            b = theirs[p][table[o * 32 + 16 + j]].astype(jnp.float32)
+            send2[p, j] = (a + b).astype(jnp.bfloat16)
+
+        cp = pltpu.make_async_remote_copy(
+            send2.at[p], recv2.at[p], s2.at[p], r2.at[p],
+            device_id=(across_y if p % 2 == 0 else across_x, h), device_id_type=MESH,
+        )
+        cp.start()
+        second.append(cp)
+
+        @pl.loop(0, 2 * depth)
+        def _(j, p=p, o=o):
+            a = mine[p, table[o * 32 + 8 + j]].astype(jnp.float32)
+            b = theirs[p][table[o * 32 + 24 + j]].astype(jnp.float32)
+            keep[p, j] = a + b
+
+    third = []
+    for p in range(chunks):
+        second[p].wait()
+        for i in range(1, depth):
+            zz = lax.rem(z + i, depth)
+            two = pl.ds(zz * 2, 2)
+            send3[p, i - 1] = (
+                keep[p, two] + recv2[p, two].astype(jnp.float32)
+            ).astype(jnp.bfloat16)
+            cp = pltpu.make_async_remote_copy(
+                send3.at[p, i - 1], recv3.at[p, i - 1], s3.at[p, i - 1], r3.at[p, i - 1],
+                device_id=(peers[i - 1], h), device_id_type=MESH,
+            )
+            cp.start()
+            third.append(cp)
+    for p in range(chunks):
+        two = pl.ds(z * 2, 2)
+        total = keep[p, two] + recv2[p, two].astype(jnp.float32)
+        for i in range(1, depth):
+            third[p * (depth - 1) + i - 1].wait()
+            total = total + recv3[p, i - 1].astype(jnp.float32)
+        for q in range(2):
+            out[q * BLOCK : (q + 1) * BLOCK, p * part : (p + 1) * part] = total[q]
+
+
+def scatter(table, term):
+    c = term.shape[1]
+    chunks = 6
+    part = c // chunks
+    bf16, f32 = jnp.bfloat16, jnp.float32
+    vmem = pl.BlockSpec(memory_space=pltpu.VMEM)
+    dma = pltpu.SemaphoreType.DMA
+    return pl.pallas_call(
+        functools.partial(scatter_kernel, chunks),
+        out_shape=jax.ShapeDtypeStruct((2 * BLOCK, c), f32),
+        in_specs=[pl.BlockSpec(memory_space=pltpu.SMEM), vmem],
+        out_specs=vmem,
+        scratch_shapes=[
+            pltpu.VMEM((chunks, LIST + 1, BLOCK, part), bf16),
+            pltpu.VMEM((chunks, 8, BLOCK, part), bf16),
+            pltpu.VMEM((chunks, 8, BLOCK, part), f32),
+            pltpu.VMEM((chunks, 8, BLOCK, part), bf16),
+            pltpu.VMEM((chunks, 3, 2, BLOCK, part), bf16),
+            pltpu.VMEM((chunks, 3, 2, BLOCK, part), bf16),
+            dma((chunks,)), dma((chunks,)), dma((chunks,)), dma((chunks,)),
+            dma((chunks, 3)), dma((chunks, 3)),
+        ]
+        + [pltpu.VMEM((LIST + 1, BLOCK, part), bf16)] * chunks,
+        compiler_params=pltpu.CompilerParams(
+            collective_id=1, has_side_effects=True, vmem_limit_bytes=48 * 2**20
+        ),
+        name="scatter",
+    )(table, term)
+
+
+def slot_table(ids):
+    me = lax.axis_index("genome")
+    x, y = me % 2, me // 2 % 2
+    slot = jnp.arange(LIST, dtype=jnp.int32)
+    j = jnp.arange(8, dtype=jnp.int32)
+
+    def where_is(lists, blocks):
+        hit = lists[None, :] == blocks[:, None]
+        return jnp.min(jnp.where(hit, slot[None, :], LIST), axis=1)
+
+    def across(bit):
+        return lax.ppermute(ids, "genome", [(g, g ^ bit) for g in range(16)])
+
+    def blocks(yy, xx):
+        return j // 2 * 8 + yy * 4 + xx * 2 + j % 2
+
+    ways = []
+    for bit, on in ((1, blocks(1 - y, x)), (2, blocks(y, 1 - x))):
+        wanted = jnp.concatenate([on, blocks(y, x)])
+        ways += [where_is(ids, wanted), where_is(across(bit), wanted)]
+    return jnp.concatenate(ways)
+
+
+def on_device(
+    features_in,
+    norm_scale,
+    norm_shift,
+    conv_weight,
+    head_weight,
+    assay_head_lists,
+    assay_list_counts,
+    targets,
+):
+    ids = assay_head_lists[0]
+    table = slot_table(ids)
+    norm = jnp.concatenate([norm_scale, norm_shift], axis=0).T
+    active = jnp.arange(LIST, dtype=jnp.int32) < assay_list_counts[0]
+    act = jnp.repeat(active.astype(jnp.float32), BLOCK)[:, None]
+    hw, tg = pick(ids, head_weight, targets.reshape(targets.shape[0], LIST * BLOCK))
+    x, term = trunk(features_in, norm, act, hw, tg, conv_weight)
+    return (x, scatter(table, term))
+
+
 def solution(mesh):
+    fits = mesh.shape["genome"] == 16 and mesh.shape["heads"] == 2
     return jax.shard_map(
-        on_device,
+        on_device if fits else on_device_general,
         mesh=mesh,
         in_specs=(
             P("heads", "genome"),

time: 383 us -> 114 us (0.30)
  waiting for transfers between devices: 248 us -> 0.01 us
  Pallas kernels: 0 us -> 99.6 us
  matrix products: 49.1 us -> 0 us
  local copies, waits for them, and re-layouts: 49.7 us -> 7.41 us
  between operations: 14.6 us -> 1.35 us
  starting transfers between devices: 12 us -> 4.52 us
  other arithmetic: 8.43 us -> 0.99 us
    reduce_scatter x1 -> x0, waiting for transfers between devices: 204 us -> none  [on_device(): lax.psum_scatter(dense, 'genome', scatter_dimension=0, tiled=True)]
    pallas_call x0 -> x3, Pallas kernels: none -> 99.6 us  [the longest x1 52.5 us: scatter(): pl.pallas_call(functools.partial(scatter_kernel, chunks), out_shape=jax.S...]
    dot_general x9 -> x0, matrix products: 49.1 us -> none  [the longest x6 37.1 us: add_taps(): jnp.dot(part_w, piece[:, k * dilation_step:k * dilation_step + rows], pre...]
    psum x1 -> x0, waiting for transfers between devices: 22.6 us -> none  [on_device(): z = lax.psum(partial_z, 'heads')]
    all_gather x2 -> x0, waiting for transfers between devices: 16.6 us -> none  [on_device(): lax.all_gather(padded_input, 'heads', axis=0, tiled=True)]
    dot_general x1 -> x0, local copies, waits for them, and re-layouts: 16.3 us -> none  [on_device(): dense = jnp.einsum('bs,stc->btc', onehot, term).reshape(TYPES, share_cols)]
    reshape x1 -> x0, local copies, waits for them, and re-layouts: 8.69 us -> none  [on_device(): blocks = head_weight.reshape(share_cols, HEAD_BLOCK_COUNT, BLOCK)]
    concatenate x1, local copies, waits for them, and re-layouts: 9.1 us -> 0.94 us  [on_device(): norm = jnp.concatenate([norm_scale, norm_shift], axis=0).T]
  transfers between devices with their start and end apart: 8 -> 2, of which waited for: 6 -> 0; matrix products, arithmetic and copies ran while one was open for 6% -> 4% of each run, Pallas kernels for 0% -> 41%
where the time goes in v1:
time: 114 us
  Pallas kernels  99.6 us (87%)
  local copies, waits for them, and re-layouts  7.41 us (6%)
  starting transfers between devices  4.52 us (4%)
  between operations  1.35 us (1%)
    pallas_call x1, Pallas kernels, scatter(): pl.pallas_call(functools.partial(scatter_kernel, chunks), out_shape=jax.S...  52.5 us
    pallas_call x1, Pallas kernels, trunk(): pl.pallas_call(trunk_kernel, out_shape=[jax.ShapeDtypeStruct((c, n), bf16...  42.5 us
    unnamed x9, local copies, waits for them, and re-layouts  5.54 us
    pallas_call x1, Pallas kernels, pick(): pl.pallas_call(pick_kernel, grid_spec=pltpu.PrefetchScalarGridSpec(num_sc...  4.58 us
    ppermute x2, starting transfers between devices, across(): return lax.ppermute(ids, 'genome', [(g, g ^ bit) for g in range(16)])  4.52 us
  transfers between devices with their start and end apart: 2, of which 0 were waited for; matrix products, arithmetic and copies ran while one was open for 4% of the time, Pallas kernels for 41%

profile of v1, /device:TPU:0, one launch (start us, length us, event | category | flops | bytes accessed | tf_op | source)
XLA Modules:
  0.0 113.8 jit_solution(16584860365238229182)
XLA Ops:
  0.6 3.0 %collective-permute-start.1 = (s32[4]{0:T(128)}, s32[4]{0:T(128)S(1)}, u32[]{:S(2)}, u32[]{:S(2)}) collective-permute-start(s32[4]{0:T(128)} %bitcast.13), channel_id=1, source_target_pairs={{0,4},{2,6},{4,0},{6,2},{8,12},{10,14},{12,8},{14,10},{16,20},{18,... | collective-permute-start | bytes 56 | tf_op jit(solution)/shard_map/ppermute | solution.py:470
  3.7 1.5 %collective-permute-start = (s32[4]{0:T(128)}, s32[4]{0:T(128)S(1)}, u32[]{:S(2)}, u32[]{:S(2)}) collective-permute-start(s32[4]{0:T(128)} %bitcast.14), channel_id=1, source_target_pairs={{0,2},{2,0},{4,6},{6,4},{8,10},{10,8},{12,14},{14,12},{16,18},{18,... | collective-permute-start | bytes 56 | tf_op jit(solution)/shard_map/ppermute | solution.py:470
  5.2 0.7 pad_maximum_fusion
  5.9 0.9 copy.17
  7.5 0.1 broadcast_in_dim.43
  7.5 0.9 copy.18.act
  8.4 2.4 %copy.21 = bf16[128,8,4,128]{3,1,2,0:T(8,128)(2,1)} copy(bf16[128,8,4,128]{3,2,1,0:T(4,128)(2,1)} %bitcast.10) | data formatting | bytes 2097152
  10.8 4.6 %pick.1 = (bf16[512,768]{1,0:T(8,128)(2,1)}, bf16[512,1024]{1,0:T(8,128)(2,1)}) custom-call(s32[4]{0:T(128)} %bitcast.15, bf16[768,4096]{1,0:T(8,128)(2,1)} %hw_ref.1, bf16[1024,512]{1,0:T(8,128)(2,1)} %bitcast.9), custom_call_target="tpu_custom_call" | custom-call | tf_op jit(solution)/shard_map/pick/pallas_call | solution.py:104
  15.4 0.0 copy-start.2
  15.4 42.5 %trunk.1 = (bf16[768,1024]{1,0:T(8,128)(2,1)}, bf16[512,768]{1,0:T(8,128)(2,1)}) custom-call(bf16[768,1024]{1,0:T(8,128)(2,1)} %feat.1, f32[768,4]{1,0:T(8,128)} %bitcast.11, f32[512,1]{1,0:T(8,128)} %copy.18.act, bf16[512,768]{1,0:T(8,128)(2,1)} %get-tuple-element.6.hw, bf16[512,1024]{1,0:T(8,128)(2,1)} %get-tuple-element.7.tg, bf16[2,3,768,1536]{3,2,1,0:T(8,128)(2,1)} %w_hbm.1), custom_call_target="tpu_custom_call" | custom-call | flops 16999999488 | bytes 20971520 | tf_op jit(solution)/shard_map/trunk/pallas_call | solution.py:310
  57.9 0.1 pad_add_fusion.1
  58.0 0.0 collective-permute-done.1
  58.0 0.0 collective-permute-done
  58.0 0.0 copy-done.2
  58.0 0.1 select_reduce_fusion.3
  58.1 0.1 pad_add_fusion.2.table
  58.2 0.0 copy-start
  58.2 1.1 copy-done
  59.3 0.0 copy-start.1
  59.3 52.5 %scatter.1 = f32[256,768]{1,0:T(8,128)S(1)} custom-call(s32[64]{0:T(128)S(1)} %pad_add_fusion.2.table, bf16[512,768]{1,0:T(8,128)(2,1)S(1)} %copy-done), custom_call_target="tpu_custom_call" | custom-call | tf_op jit(solution)/shard_map/scatter/pallas_call | solution.py:436
  111.8 0.0 copy-done.1
  111.8 1.1 %copy.25 = bf16[768,1024]{1,0:T(8,128)(2,1)} copy(bf16[768,1024]{1,0:T(8,128)(2,1)S(1)} %copy-done.1) | data formatting | bytes 3145728
  113.0 0.9 copy.26
  (3 shorter events, 0.0 us)
Async XLA Ops:
  0.6 57.4 %collective-permute-start.1 = (s32[4]{0:T(128)}, s32[4]{0:T(128)S(1)}, u32[]{:S(2)}, u32[]{:S(2)}) collective-permute-start(s32[4]{0:T(128)} %bitcast.13), channel_id=1, source_target_pairs={{0,4},{2,6},{4,0},{6,2},{8,12},{10,14},{12,8},{14,10},{16,20},{18,... | collective-permute-start | bytes 56 | tf_op jit(solution)/shard_map/ppermute | solution.py:470
  3.7 54.3 %collective-permute-start = (s32[4]{0:T(128)}, s32[4]{0:T(128)S(1)}, u32[]{:S(2)}, u32[]{:S(2)}) collective-permute-start(s32[4]{0:T(128)} %bitcast.14), channel_id=1, source_target_pairs={{0,2},{2,0},{4,6},{6,4},{8,10},{10,8},{12,14},{14,12},{16,18},{18,... | collective-permute-start | bytes 56 | tf_op jit(solution)/shard_map/ppermute | solution.py:470
  15.4 42.6 %copy-start.2 = (s32[1,4]{1,0:T(1,128)S(1)}, s32[1,4]{1,0:T(1,128)}, u32[]{:S(2)}) copy-start(s32[1,4]{1,0:T(1,128)} %param.13) | copy-start | bytes 52
  58.2 1.1 copy-start
  59.3 52.5 %copy-start.1 = (bf16[768,1024]{1,0:T(8,128)(2,1)S(1)}, bf16[768,1024]{1,0:T(8,128)(2,1)}, u32[]{:S(2)}) copy-start(bf16[768,1024]{1,0:T(8,128)(2,1)} %get-tuple-element.20) | copy-start | bytes 4718596

commit v2 on v1

--- a/solution.py
+++ b/solution.py
@@ -93,41 +93,30 @@
     return 0.5 * v * (1.0 + lax.erf(v * 0.7071067811865476))
 
 
-def pick_kernel(ids_ref, hw_ref, tg_ref, hw_out, tg_out):
+def pick_kernel(ids_ref, hw_ref, hw_out):
     hw_out[...] = hw_ref[...].T
-    tg_out[...] = tg_ref[...].T
-
-
-def pick(ids, head_weight, goal):
+
+
+def pick(ids, head_weight):
     c = head_weight.shape[0]
-    n = goal.shape[0]
     return pl.pallas_call(
         pick_kernel,
         grid_spec=pltpu.PrefetchScalarGridSpec(
             num_scalar_prefetch=1,
             grid=(LIST,),
-            in_specs=[
-                pl.BlockSpec((c, BLOCK), lambda s, ids: (0, ids[s])),
-                pl.BlockSpec((n, BLOCK), lambda s, ids: (0, s)),
-            ],
-            out_specs=[
-                pl.BlockSpec((BLOCK, c), lambda s, ids: (s, 0)),
-                pl.BlockSpec((BLOCK, n), lambda s, ids: (s, 0)),
-            ],
+            in_specs=[pl.BlockSpec((c, BLOCK), lambda s, ids: (0, ids[s]))],
+            out_specs=pl.BlockSpec((BLOCK, c), lambda s, ids: (s, 0)),
         ),
-        out_shape=[
-            jax.ShapeDtypeStruct((LIST * BLOCK, c), jnp.bfloat16),
-            jax.ShapeDtypeStruct((LIST * BLOCK, n), jnp.bfloat16),
-        ],
+        out_shape=jax.ShapeDtypeStruct((LIST * BLOCK, c), jnp.bfloat16),
         name="pick",
-    )(ids, head_weight, goal)
+    )(ids, head_weight)
 
 
 def trunk_kernel(
-    feat, norm, act, hw, tg, w_hbm,
-    x_out, term,
+    feat, norm, act, ids, hw, goal, w_hbm,
+    x_out, term, lists,
     w, xe, u, r, acc, edge_out, edge_in, z_own, z_out, z_in,
-    w_sem, edge_send, edge_recv, u_send, u_recv, z_send, z_recv,
+    tg, w_sem, edge_send, edge_recv, u_send, u_recv, z_send, z_recv, id_send, id_recv,
 ):
     c, n = feat.shape
     wide = n + HALO
@@ -146,14 +135,17 @@
             loads.append(cp)
 
     barrier = pltpu.get_barrier_semaphore()
-    for dev in ((me, other), (left, h), (right, h)):
+    near = [(flip(me, bit), h) for bit in NEAR]
+    for dev in [(me, other), (left, h), (right, h)] + near:
         pl.semaphore_signal(barrier, inc=1, device_id=dev, device_id_type=MESH)
 
     edge_out[0] = feat[:, 0:BLOCK].astype(jnp.float32).T[:EDGE].astype(jnp.bfloat16)
     edge_out[1] = (
         feat[:, n - BLOCK : n].astype(jnp.float32).T[BLOCK - EDGE :].astype(jnp.bfloat16)
     )
-    pl.semaphore_wait(barrier, 3)
+    for s in range(LIST):
+        tg[s * BLOCK : (s + 1) * BLOCK, :] = goal[:, s * BLOCK : (s + 1) * BLOCK].T
+    pl.semaphore_wait(barrier, 3 + len(near))
     edges = []
     for i, dev in enumerate((left, right)):
         cp = pltpu.make_async_remote_copy(
@@ -162,6 +154,14 @@
         )
         cp.start()
         edges.append(cp)
+    asked = []
+    for i, dev in enumerate(near):
+        cp = pltpu.make_async_remote_copy(
+            ids, lists.at[i], id_send.at[i], id_recv.at[i],
+            device_id=dev, device_id_type=MESH,
+        )
+        cp.start()
+        asked.append(cp)
 
     lane = lax.broadcasted_iota(jnp.int32, (1, wide), 1)
     inside = jnp.where(
@@ -190,18 +190,32 @@
         r[layer, half, 0, rows, :] = pltpu.roll(val, d, 1).astype(jnp.bfloat16)
         r[layer, half, 1, rows, :] = pltpu.roll(val, wide - d, 1).astype(jnp.bfloat16)
 
+    def active(layer, rows, v, mask):
+        a = norm[rows, layer : layer + 1]
+        b = norm[rows, LAYERS + layer : LAYERS + layer + 1]
+        val = gelu(v.astype(jnp.float32) * a + b)
+        return (val if mask is None else val * mask).astype(jnp.bfloat16)
+
     def activate(layer, m):
         @pl.loop(0, step // BLOCK)
         def _(j):
             rows = pl.ds(pl.multiple_of(m * step + j * BLOCK, BLOCK), BLOCK)
-            v = xe[layer, rows, :].astype(jnp.float32)
-            a = norm[rows, layer : layer + 1]
-            b = norm[rows, LAYERS + layer : LAYERS + layer + 1]
-            val = (gelu(v * a + b) * inside).astype(jnp.bfloat16)
+            val = active(layer, rows, xe[layer, rows, :], inside)
             u[layer, 0, rows, :] = val
-            shifted(layer, 0, rows, val.astype(jnp.float32))
-
-    xe[0, :, 0:n] = feat[...]
+
+    def shift_own(layer):
+        @pl.loop(0, c // BLOCK)
+        def _(j):
+            rows = pl.ds(pl.multiple_of(j * BLOCK, BLOCK), BLOCK)
+            shifted(layer, 0, rows, u[layer, 0, rows, :].astype(jnp.float32))
+
+    @pl.loop(0, c // BLOCK)
+    def _(j):
+        rows = pl.ds(pl.multiple_of(j * BLOCK, BLOCK), BLOCK)
+        val = feat[rows, :]
+        xe[0, rows, 0:n] = val
+        u[0, 0, rows, 0:n] = active(0, rows, val, None)
+
     for cp in edges:
         cp.wait()
     halo = jnp.concatenate(
@@ -212,7 +226,9 @@
         ],
         axis=0,
     )
-    xe[0, :, n:wide] = halo.T.astype(jnp.bfloat16)
+    halo = halo.T
+    xe[0, :, n:wide] = halo.astype(jnp.bfloat16)
+    u[0, 0, :, n:wide] = active(0, slice(None), halo, inside[:, n:wide])
 
     def own_part(layer, m, width):
         rows = pl.ds(pl.multiple_of(m * step, step), step)
@@ -232,7 +248,6 @@
 
     copies = []
     for m in range(pieces):
-        activate(0, m)
         cp = u_copy(0, m)
         cp.start()
         copies.append(cp)
@@ -240,6 +255,7 @@
     for layer in range(LAYERS):
         last = layer == LAYERS - 1
         width = n if last else wide
+        shift_own(layer)
         for k in range(3):
             loads[3 * layer + k].wait()
 
@@ -300,9 +316,11 @@
         term[rows, :] = lax.dot_general(
             slope, x_out[...], (((1,), (1,)), ((), ())), preferred_element_type=jnp.float32
         ).astype(jnp.bfloat16)
-
-
-def trunk(feat, norm, act, hw, tg, w):
+    for cp in asked:
+        cp.wait()
+
+
+def trunk(feat, norm, act, ids, hw, goal, w):
     c, n = feat.shape
     wide = n + HALO
     vmem = pl.BlockSpec(memory_space=pltpu.VMEM)
@@ -312,9 +330,10 @@
         out_shape=[
             jax.ShapeDtypeStruct((c, n), bf16),
             jax.ShapeDtypeStruct((LIST * BLOCK, c), bf16),
+            jax.ShapeDtypeStruct((len(NEAR),) + ids.shape, jnp.int32),
         ],
-        in_specs=[vmem] * 5 + [pl.BlockSpec(memory_space=pl.ANY)],
-        out_specs=[vmem, vmem],
+        in_specs=[vmem] * 6 + [pl.BlockSpec(memory_space=pl.ANY)],
+        out_specs=[vmem, vmem, vmem],
         scratch_shapes=[
             pltpu.VMEM(w.shape, bf16),
             pltpu.VMEM((LAYERS, c, wide), bf16),
@@ -326,6 +345,7 @@
             pltpu.VMEM((LIST * BLOCK, n), f32),
             pltpu.VMEM((LIST * BLOCK, n), bf16),
             pltpu.VMEM((LIST * BLOCK, n), bf16),
+            pltpu.VMEM((LIST * BLOCK, n), bf16),
             pltpu.SemaphoreType.DMA((LAYERS, 3)),
             pltpu.SemaphoreType.DMA((2,)),
             pltpu.SemaphoreType.DMA((2,)),
@@ -333,6 +353,8 @@
             pltpu.SemaphoreType.DMA((LAYERS, 3)),
             pltpu.SemaphoreType.DMA((2,)),
             pltpu.SemaphoreType.DMA((2,)),
+            pltpu.SemaphoreType.DMA((len(NEAR),)),
+            pltpu.SemaphoreType.DMA((len(NEAR),)),
         ],
         compiler_params=pltpu.CompilerParams(
             collective_id=0, has_side_effects=True, vmem_limit_bytes=60 * 2**20
@@ -341,113 +363,132 @@
             flops=17 * 10**9, bytes_accessed=20 * 2**20, transcendentals=0
         ),
         name="trunk",
-    )(feat, norm, act, hw, tg, w)
+    )(feat, norm, act, ids, hw, goal, w)
+
+
+ORDERS = ((1, 2, 4), (2, 1, 4), (4, 1, 2), (4, 2, 1))
+CHUNKS = (0, 1, 2, 0, 1, 3)
+NEAR = (1, 2, 4)
+
+
+def flip(index, bit):
+    return index + bit - 2 * bit * lax.rem(index // bit, 2)
 
 
 def scatter_kernel(
-    chunks, table, term, out,
-    mine, send2, keep, recv2, send3, recv3,
-    s1, r1, s2, r2, s3, r3,
+    table, term, out,
+    mine, send2, keep2, recv2, send3, keep3, recv3, send4, keep4, recv4,
+    s1, r1, s2, r2, s3, r3, s4, r4,
     *theirs,
 ):
     me = lax.axis_index("genome")
     h = lax.axis_index("heads")
-    x, y, z = lax.rem(me, 2), lax.rem(me // 2, 2), me // 4
-    depth = lax.axis_size("genome") // 4
-    across_x = (z * 2 + y) * 2 + (1 - x)
-    across_y = (z * 2 + (1 - y)) * 2 + x
+    chunks = len(CHUNKS)
     part = mine.shape[-1]
+    f32, bf16 = jnp.float32, jnp.bfloat16
 
     barrier = pltpu.get_barrier_semaphore()
-    peers = [lax.rem(z + i, depth) * 4 + y * 2 + x for i in range(1, depth)]
-    for dev in [across_x, across_y] + peers:
-        pl.semaphore_signal(barrier, inc=1, device_id=(dev, h), device_id_type=MESH)
+    for bit in NEAR + (8,):
+        pl.semaphore_signal(barrier, inc=1, device_id=(flip(me, bit), h), device_id_type=MESH)
     for p in range(chunks):
         for s in range(LIST):
             mine[p, s] = term[s * BLOCK : (s + 1) * BLOCK, p * part : (p + 1) * part]
-        mine[p, LIST] = jnp.zeros((BLOCK, part), jnp.bfloat16)
-        theirs[p][LIST] = jnp.zeros((BLOCK, part), jnp.bfloat16)
-    pl.semaphore_wait(barrier, 2 + len(peers))
-
-    first = []
+        mine[p, LIST] = jnp.zeros((BLOCK, part), bf16)
+        theirs[p][LIST] = jnp.zeros((BLOCK, part), bf16)
+    pl.semaphore_wait(barrier, len(NEAR) + 1)
+
+    def send(src, dst, send_sem, recv_sem, bit):
+        cp = pltpu.make_async_remote_copy(
+            src, dst, send_sem, recv_sem, device_id=(flip(me, bit), h), device_id_type=MESH
+        )
+        cp.start()
+        return cp
+
+    first, second, third, fourth = {}, {}, {}, {}
     for p in range(chunks):
-        cp = pltpu.make_async_remote_copy(
+        first[p] = send(
             mine.at[p, pl.ds(0, LIST)], theirs[p].at[pl.ds(0, LIST)], s1.at[p], r1.at[p],
-            device_id=(across_x if p % 2 == 0 else across_y, h), device_id_type=MESH,
-        )
-        cp.start()
-        first.append(cp)
-    second = []
-    for p in range(chunks):
+            ORDERS[CHUNKS[p]][0],
+        )
+
+    def stage2(p):
+        base = CHUNKS[p] * 32
         first[p].wait()
-        o = p % 2
-
-        @pl.loop(0, 2 * depth)
-        def _(j, p=p, o=o):
-            a = mine[p, table[o * 32 + j]].astype(jnp.float32)
-            b = theirs[p][table[o * 32 + 16 + j]].astype(jnp.float32)
-            send2[p, j] = (a + b).astype(jnp.bfloat16)
-
-        cp = pltpu.make_async_remote_copy(
-            send2.at[p], recv2.at[p], s2.at[p], r2.at[p],
-            device_id=(across_y if p % 2 == 0 else across_x, h), device_id_type=MESH,
-        )
-        cp.start()
-        second.append(cp)
-
-        @pl.loop(0, 2 * depth)
-        def _(j, p=p, o=o):
-            a = mine[p, table[o * 32 + 8 + j]].astype(jnp.float32)
-            b = theirs[p][table[o * 32 + 24 + j]].astype(jnp.float32)
-            keep[p, j] = a + b
-
-    third = []
-    for p in range(chunks):
+
+        def both(j):
+            x = mine[p, table[base + j]].astype(f32)
+            return x + theirs[p][table[base + 16 + j]].astype(f32)
+
+        @pl.loop(0, 8)
+        def _(j):
+            send2[p, j] = both(j).astype(bf16)
+
+        second[p] = send(
+            send2.at[p], recv2.at[p], s2.at[p], r2.at[p], ORDERS[CHUNKS[p]][1]
+        )
+
+        @pl.loop(0, 8)
+        def _(j):
+            keep2[p, j] = both(8 + j)
+
+    def stage3(p):
         second[p].wait()
-        for i in range(1, depth):
-            zz = lax.rem(z + i, depth)
-            two = pl.ds(zz * 2, 2)
-            send3[p, i - 1] = (
-                keep[p, two] + recv2[p, two].astype(jnp.float32)
-            ).astype(jnp.bfloat16)
-            cp = pltpu.make_async_remote_copy(
-                send3.at[p, i - 1], recv3.at[p, i - 1], s3.at[p, i - 1], r3.at[p, i - 1],
-                device_id=(peers[i - 1], h), device_id_type=MESH,
+
+        @pl.loop(0, 4)
+        def _(j):
+            send3[p, j] = (keep2[p, j] + recv2[p, j].astype(f32)).astype(bf16)
+
+        third[p] = send(
+            send3.at[p], recv3.at[p], s3.at[p], r3.at[p], ORDERS[CHUNKS[p]][2]
+        )
+
+        @pl.loop(0, 4)
+        def _(j):
+            keep3[p, j] = keep2[p, 4 + j] + recv2[p, 4 + j].astype(f32)
+
+    def stage4(p):
+        third[p].wait()
+        for j in range(2):
+            send4[p, j] = (keep3[p, j] + recv3[p, j].astype(f32)).astype(bf16)
+        fourth[p] = send(send4.at[p], recv4.at[p], s4.at[p], r4.at[p], 8)
+        for j in range(2):
+            keep4[p, j] = keep3[p, 2 + j] + recv3[p, 2 + j].astype(f32)
+
+    def finish(p):
+        fourth[p].wait()
+        for j in range(2):
+            out[j * BLOCK : (j + 1) * BLOCK, p * part : (p + 1) * part] = (
+                keep4[p, j] + recv4[p, j].astype(f32)
             )
-            cp.start()
-            third.append(cp)
-    for p in range(chunks):
-        two = pl.ds(z * 2, 2)
-        total = keep[p, two] + recv2[p, two].astype(jnp.float32)
-        for i in range(1, depth):
-            third[p * (depth - 1) + i - 1].wait()
-            total = total + recv3[p, i - 1].astype(jnp.float32)
-        for q in range(2):
-            out[q * BLOCK : (q + 1) * BLOCK, p * part : (p + 1) * part] = total[q]
+
+    for t in range(chunks + 3):
+        for lag, stage in enumerate((stage2, stage3, stage4, finish)):
+            if 0 <= t - lag < chunks:
+                stage(t - lag)
 
 
 def scatter(table, term):
     c = term.shape[1]
-    chunks = 6
+    chunks = len(CHUNKS)
     part = c // chunks
     bf16, f32 = jnp.bfloat16, jnp.float32
     vmem = pl.BlockSpec(memory_space=pltpu.VMEM)
-    dma = pltpu.SemaphoreType.DMA
+
+    def buf(count, kind):
+        return pltpu.VMEM((chunks, count, BLOCK, part), kind)
+
     return pl.pallas_call(
-        functools.partial(scatter_kernel, chunks),
+        scatter_kernel,
         out_shape=jax.ShapeDtypeStruct((2 * BLOCK, c), f32),
         in_specs=[pl.BlockSpec(memory_space=pltpu.SMEM), vmem],
         out_specs=vmem,
         scratch_shapes=[
-            pltpu.VMEM((chunks, LIST + 1, BLOCK, part), bf16),
-            pltpu.VMEM((chunks, 8, BLOCK, part), bf16),
-            pltpu.VMEM((chunks, 8, BLOCK, part), f32),
-            pltpu.VMEM((chunks, 8, BLOCK, part), bf16),
-            pltpu.VMEM((chunks, 3, 2, BLOCK, part), bf16),
-            pltpu.VMEM((chunks, 3, 2, BLOCK, part), bf16),
-            dma((chunks,)), dma((chunks,)), dma((chunks,)), dma((chunks,)),
-            dma((chunks, 3)), dma((chunks, 3)),
+            buf(LIST + 1, bf16),
+            buf(8, bf16), buf(8, f32), buf(8, bf16),
+            buf(4, bf16), buf(4, f32), buf(4, bf16),
+            buf(2, bf16), buf(2, f32), buf(2, bf16),
         ]
+        + [pltpu.SemaphoreType.DMA((chunks,))] * 8
         + [pltpu.VMEM((LIST + 1, BLOCK, part), bf16)] * chunks,
         compiler_params=pltpu.CompilerParams(
             collective_id=1, has_side_effects=True, vmem_limit_bytes=48 * 2**20
@@ -456,27 +497,20 @@
     )(table, term)
 
 
-def slot_table(ids):
+def slot_table(lists):
     me = lax.axis_index("genome")
-    x, y = me % 2, me // 2 % 2
+    j = jnp.arange(16, dtype=jnp.int32)
     slot = jnp.arange(LIST, dtype=jnp.int32)
-    j = jnp.arange(8, dtype=jnp.int32)
-
-    def where_is(lists, blocks):
-        hit = lists[None, :] == blocks[:, None]
-        return jnp.min(jnp.where(hit, slot[None, :], LIST), axis=1)
-
-    def across(bit):
-        return lax.ppermute(ids, "genome", [(g, g ^ bit) for g in range(16)])
-
-    def blocks(yy, xx):
-        return j // 2 * 8 + yy * 4 + xx * 2 + j % 2
-
-    ways = []
-    for bit, on in ((1, blocks(1 - y, x)), (2, blocks(y, 1 - x))):
-        wanted = jnp.concatenate([on, blocks(y, x)])
-        ways += [where_is(ids, wanted), where_is(across(bit), wanted)]
-    return jnp.concatenate(ways)
+    owners = []
+    for one, two, three in ORDERS:
+        change = (1 - j // 8) * two + (1 - j // 4 % 2) * three + (1 - j // 2 % 2) * 8
+        owners.append((me ^ change) * 2 + j % 2)
+    owners = jnp.stack(owners)
+    pairs = jnp.stack(
+        [jnp.stack([lists[0], lists[1 + NEAR.index(order[0])]]) for order in ORDERS]
+    )
+    hit = pairs[:, :, None, :] == owners[:, None, :, None]
+    return jnp.min(jnp.where(hit, slot, LIST), axis=-1).reshape(-1)
 
 
 def on_device(
@@ -490,12 +524,14 @@
     targets,
 ):
     ids = assay_head_lists[0]
-    table = slot_table(ids)
     norm = jnp.concatenate([norm_scale, norm_shift], axis=0).T
     active = jnp.arange(LIST, dtype=jnp.int32) < assay_list_counts[0]
     act = jnp.repeat(active.astype(jnp.float32), BLOCK)[:, None]
-    hw, tg = pick(ids, head_weight, targets.reshape(targets.shape[0], LIST * BLOCK))
-    x, term = trunk(features_in, norm, act, hw, tg, conv_weight)
+    hw = pick(ids, head_weight)
+    goal = targets.reshape(targets.shape[0], LIST * BLOCK)
+    own = jnp.pad(assay_head_lists, ((0, 7), (0, BLOCK - LIST)))
+    x, term, lists = trunk(features_in, norm, act, own, hw, goal, conv_weight)
+    table = slot_table(jnp.concatenate([ids[None], lists[:, 0, :LIST]]))
     return (x, scatter(table, term))
 
 

time: 114 us -> 105 us (0.921)
  Pallas kernels: 99.6 us -> 93.9 us
  starting transfers between devices: 4.52 us -> 0 us
  local copies, waits for them, and re-layouts: 7.41 us -> 8.81 us
    pallas_call x1, Pallas kernels: 52.5 us -> 45.2 us  [scatter(): pl.pallas_call(scatter_kernel, out_shape=jax.ShapeDtypeStruct((2 * BLOCK,...]
    ppermute x2 -> x0, starting transfers between devices: 4.52 us -> none  [across(): return lax.ppermute(ids, 'genome', [(g, g ^ bit) for g in range(16)])]
    pallas_call x1, Pallas kernels: 42.5 us -> 44.4 us  [trunk(): pl.pallas_call(trunk_kernel, out_shape=[jax.ShapeDtypeStruct((c, n), bf16...]
    unnamed x9 -> x13, local copies, waits for them, and re-layouts: 5.54 us -> 5.55 us
  transfers between devices with their start and end apart: 2 -> 0, of which waited for: 0 -> 0; matrix products, arithmetic and copies ran while one was open for 4% -> 0% of each run, Pallas kernels for 41% -> 0%
where the time goes in v2:
time: 105 us; the launch traced here: 104 us
  Pallas kernels  93.9 us (89%)
  local copies, waits for them, and re-layouts  8.81 us (8%)
  between operations  1.36 us (1%)
    pallas_call x1, Pallas kernels, scatter(): pl.pallas_call(scatter_kernel, out_shape=jax.ShapeDtypeStruct((2 * BLOCK,...  45.2 us
    pallas_call x1, Pallas kernels, trunk(): pl.pallas_call(trunk_kernel, out_shape=[jax.ShapeDtypeStruct((c, n), bf16...  44.4 us
    unnamed x13, local copies, waits for them, and re-layouts  5.55 us
    pallas_call x1, Pallas kernels, pick(): pl.pallas_call(pick_kernel, grid_spec=pltpu.PrefetchScalarGridSpec(num_sc...  4.24 us

profile of v2, /device:TPU:0, one launch (start us, length us, event | category | flops | bytes accessed | tf_op | source)
XLA Modules:
  0.0 104.2 jit_solution(7845971488035039207)
XLA Ops:
  0.6 2.4 %copy.21 = bf16[128,8,4,128]{3,1,2,0:T(8,128)(2,1)} copy(bf16[128,8,4,128]{3,2,1,0:T(4,128)(2,1)} %bitcast.21) | data formatting | bytes 2097152
  3.0 0.0 copy-start.2
  3.0 0.0 copy-start.3
  3.0 0.0 copy-start.4
  3.0 4.2 %pick.1.hw = bf16[512,768]{1,0:T(8,128)(2,1)} custom-call(s32[4]{0:T(128)} %bitcast.25, bf16[768,4096]{1,0:T(8,128)(2,1)} %hw_ref.1), custom_call_target="tpu_custom_call" | custom-call | tf_op jit(solution)/shard_map/pick/pallas_call | solution.py:102
  7.3 0.0 copy-done.2
  7.3 0.0 copy-done.3
  7.3 0.9 copy.17
  8.9 0.1 broadcast_in_dim.13
  8.9 0.9 copy.18.act
  9.8 0.0 copy-done.4
  9.8 0.6 pad.4.ids
  10.4 44.4 %trunk.1 = (bf16[768,1024]{1,0:T(8,128)(2,1)}, bf16[512,768]{1,0:T(8,128)(2,1)}, s32[3,8,128]{2,1,0:T(8,128)}) custom-call(bf16[768,1024]{1,0:T(8,128)(2,1)} %feat.1, f32[768,4]{1,0:T(8,128)} %bitcast.23, f32[512,1]{1,0:T(8,128)} %copy.18.act, s32[8,128]{1,0:T(8,128)} %pad.4.ids, bf16[512,768]{1,0:T(8,128)(2,1)} %pick.1.hw, bf16[1024,512]{1,0:T(8,128)(2,1)} %bitcast.22, ...), custom_call_target="tpu_custom_call" | custom-call | flops 16999999488 | bytes 20971520 | tf_op jit(solution)/shard_map/trunk/pallas_call | solution.py:328
  54.9 0.7 slice_bitcast_fusion.2
  55.7 0.1 select_reduce_fusion
  55.8 0.1 reshape.263.table
  55.8 0.0 copy-start
  55.9 1.1 %copy-done = bf16[512,768]{1,0:T(8,128)(2,1)S(1)} copy-done((bf16[512,768]{1,0:T(8,128)(2,1)S(1)}, bf16[512,768]{1,0:T(8,128)(2,1)}, u32[]{:S(2)}) %copy-start) | copy-done | bytes 786456
  57.0 0.0 copy-start.1
  57.0 45.2 %scatter.1 = f32[256,768]{1,0:T(8,128)S(1)} custom-call(s32[128]{0:T(128)S(1)} %reshape.263.table, bf16[512,768]{1,0:T(8,128)(2,1)S(1)} %copy-done), custom_call_target="tpu_custom_call" | custom-call | tf_op jit(solution)/shard_map/scatter/pallas_call | solution.py:480
  102.2 0.0 copy-done.1
  102.2 1.1 %copy.25 = bf16[768,1024]{1,0:T(8,128)(2,1)} copy(bf16[768,1024]{1,0:T(8,128)(2,1)S(1)} %copy-done.1) | data formatting | bytes 3145728
  103.4 0.9 copy.26
  (7 shorter events, 0.1 us)
Async XLA Ops:
  3.0 4.3 %copy-start.2 = (f32[2,768]{1,0:T(2,128)S(1)}, f32[2,768]{1,0:T(2,128)}, u32[]{:S(2)}) copy-start(f32[2,768]{1,0:T(2,128)} %param.10) | copy-start | bytes 18436
  3.0 4.3 %copy-start.3 = (f32[2,768]{1,0:T(2,128)S(1)}, f32[2,768]{1,0:T(2,128)}, u32[]{:S(2)}) copy-start(f32[2,768]{1,0:T(2,128)} %param.9) | copy-start | bytes 18436
  3.0 6.8 %copy-start.4 = (s32[1,4]{1,0:T(1,128)S(1)}, s32[1,4]{1,0:T(1,128)}, u32[]{:S(2)}) copy-start(s32[1,4]{1,0:T(1,128)} %param.13) | copy-start | bytes 52
  55.8 1.1 %copy-start = (bf16[512,768]{1,0:T(8,128)(2,1)S(1)}, bf16[512,768]{1,0:T(8,128)(2,1)}, u32[]{:S(2)}) copy-start(bf16[512,768]{1,0:T(8,128)(2,1)} %get-tuple-element.7.term) | copy-start | bytes 2359300
  57.0 45.2 %copy-start.1 = (bf16[768,1024]{1,0:T(8,128)(2,1)S(1)}, bf16[768,1024]{1,0:T(8,128)(2,1)}, u32[]{:S(2)}) copy-start(bf16[768,1024]{1,0:T(8,128)(2,1)} %get-tuple-element.20) | copy-start | bytes 4718596

commit v3 on v2

--- a/solution.py
+++ b/solution.py
@@ -93,8 +93,10 @@
     return 0.5 * v * (1.0 + lax.erf(v * 0.7071067811865476))
 
 
-def pick_kernel(ids_ref, hw_ref, hw_out):
-    hw_out[...] = hw_ref[...].T
+def pick_kernel(ids_ref, *refs):
+    hw_out = refs[LIST]
+    for s in range(LIST):
+        hw_out[s * BLOCK : (s + 1) * BLOCK, :] = refs[s][...].T
 
 
 def pick(ids, head_weight):
@@ -103,19 +105,22 @@
         pick_kernel,
         grid_spec=pltpu.PrefetchScalarGridSpec(
             num_scalar_prefetch=1,
-            grid=(LIST,),
-            in_specs=[pl.BlockSpec((c, BLOCK), lambda s, ids: (0, ids[s]))],
-            out_specs=pl.BlockSpec((BLOCK, c), lambda s, ids: (s, 0)),
+            grid=(1,),
+            in_specs=[
+                pl.BlockSpec((c, BLOCK), functools.partial(lambda s, i, ids: (0, ids[s]), s))
+                for s in range(LIST)
+            ],
+            out_specs=pl.BlockSpec((LIST * BLOCK, c), lambda i, ids: (0, 0)),
         ),
         out_shape=jax.ShapeDtypeStruct((LIST * BLOCK, c), jnp.bfloat16),
         name="pick",
-    )(ids, head_weight)
+    )(ids, *[head_weight] * LIST)
 
 
 def trunk_kernel(
     feat, norm, act, ids, hw, goal, w_hbm,
     x_out, term, lists,
-    w, xe, u, r, acc, edge_out, edge_in, z_own, z_out, z_in,
+    w, xe, u, acc, edge_out, edge_in, z_own, z_out, z_in,
     tg, w_sem, edge_send, edge_recv, u_send, u_recv, z_send, z_recv, id_send, id_recv,
 ):
     c, n = feat.shape
@@ -129,10 +134,15 @@
 
     loads = []
     for layer in range(LAYERS):
-        for k in range(3):
-            cp = pltpu.make_async_copy(w_hbm.at[layer, k], w.at[layer, k], w_sem.at[layer, k])
-            cp.start()
-            loads.append(cp)
+        for side, start in enumerate((h, other)):
+            for k in range(3):
+                cp = pltpu.make_async_copy(
+                    w_hbm.at[layer, k, :, pl.ds(pl.multiple_of(start * c, c), c)],
+                    w.at[layer, side, :, pl.ds(k * c, c)],
+                    w_sem.at[layer, side, k],
+                )
+                cp.start()
+                loads.append(cp)
 
     barrier = pltpu.get_barrier_semaphore()
     near = [(flip(me, bit), h) for bit in NEAR]
@@ -177,18 +187,30 @@
     pieces = 3
     step = c // pieces
 
+    tiles = [(0, n // 2), (n // 2, n // 2), (n, HALO)]
+
     def u_copy(layer, m):
-        rows = pl.ds(m * step, step)
+        if layer == 0:
+            part = (pl.ds(c + m * step, step), slice(None))
+        else:
+            part = (pl.ds(c, c), pl.ds(*tiles[m]))
         return pltpu.make_async_remote_copy(
-            u.at[layer, 0, rows], u.at[layer, 1, rows],
+            u.at[(layer, 0) + part], u.at[(layer, 1) + part],
             u_send.at[layer, m], u_recv.at[layer, m],
             device_id=(me, other), device_id_type=MESH,
         )
 
-    def shifted(layer, half, rows, val):
+    def shift(layer, side):
         d = BASE_DILATION * 2**layer
-        r[layer, half, 0, rows, :] = pltpu.roll(val, d, 1).astype(jnp.bfloat16)
-        r[layer, half, 1, rows, :] = pltpu.roll(val, wide - d, 1).astype(jnp.bfloat16)
+
+        @pl.loop(0, c // BLOCK)
+        def _(j):
+            def rows(k):
+                return pl.ds(pl.multiple_of(k * c + j * BLOCK, BLOCK), BLOCK)
+
+            val = u[layer, side, rows(1), :].astype(jnp.float32)
+            u[layer, side, rows(0), :] = pltpu.roll(val, d, 1).astype(jnp.bfloat16)
+            u[layer, side, rows(2), :] = pltpu.roll(val, wide - d, 1).astype(jnp.bfloat16)
 
     def active(layer, rows, v, mask):
         a = norm[rows, layer : layer + 1]
@@ -196,25 +218,29 @@
         val = gelu(v.astype(jnp.float32) * a + b)
         return (val if mask is None else val * mask).astype(jnp.bfloat16)
 
-    def activate(layer, m):
-        @pl.loop(0, step // BLOCK)
-        def _(j):
-            rows = pl.ds(pl.multiple_of(m * step + j * BLOCK, BLOCK), BLOCK)
-            val = active(layer, rows, xe[layer, rows, :], inside)
-            u[layer, 0, rows, :] = val
-
-    def shift_own(layer):
+    def activate(layer, lanes):
+        start, size = lanes
+
         @pl.loop(0, c // BLOCK)
         def _(j):
             rows = pl.ds(pl.multiple_of(j * BLOCK, BLOCK), BLOCK)
-            shifted(layer, 0, rows, u[layer, 0, rows, :].astype(jnp.float32))
+            u[layer, 0, pl.ds(pl.multiple_of(c + j * BLOCK, BLOCK), BLOCK), pl.ds(start, size)] = (
+                active(
+                    layer,
+                    rows,
+                    xe[layer, rows, pl.ds(start, size)],
+                    inside[:, start:] if start == n else None,
+                )
+            )
 
     @pl.loop(0, c // BLOCK)
     def _(j):
         rows = pl.ds(pl.multiple_of(j * BLOCK, BLOCK), BLOCK)
         val = feat[rows, :]
         xe[0, rows, 0:n] = val
-        u[0, 0, rows, 0:n] = active(0, rows, val, None)
+        u[0, 0, pl.ds(pl.multiple_of(c + j * BLOCK, BLOCK), BLOCK), 0:n] = active(
+            0, rows, val, None
+        )
 
     for cp in edges:
         cp.wait()
@@ -228,23 +254,7 @@
     )
     halo = halo.T
     xe[0, :, n:wide] = halo.astype(jnp.bfloat16)
-    u[0, 0, :, n:wide] = active(0, slice(None), halo, inside[:, n:wide])
-
-    def own_part(layer, m, width):
-        rows = pl.ds(pl.multiple_of(m * step, step), step)
-        cols = pl.ds(pl.multiple_of(h * c, c), c)
-        t = dot(w[layer, 0, rows, cols], r[layer, 0, 0, :, 0:width])
-        t = t + dot(w[layer, 1, rows, cols], u[layer, 0, :, 0:width])
-        t = t + dot(w[layer, 2, rows, cols], r[layer, 0, 1, :, 0:width])
-        acc[rows, 0:width] = t
-
-    def other_part(layer, m, width):
-        rows = pl.ds(pl.multiple_of(m * step, step), step)
-        cols = pl.ds(pl.multiple_of(other * c, c), c)
-        t = acc[rows, 0:width] + dot(w[layer, 0, rows, cols], r[layer, 1, 0, :, 0:width])
-        t = t + dot(w[layer, 1, rows, cols], u[layer, 1, :, 0:width])
-        t = t + dot(w[layer, 2, rows, cols], r[layer, 1, 1, :, 0:width])
-        return rows, (xe[layer, rows, 0:width].astype(jnp.float32) + t).astype(jnp.bfloat16)
+    u[0, 0, c : 2 * c, n:wide] = active(0, slice(None), halo, inside[:, n:wide])
 
     copies = []
     for m in range(pieces):
@@ -254,37 +264,29 @@
 
     for layer in range(LAYERS):
         last = layer == LAYERS - 1
-        width = n if last else wide
-        shift_own(layer)
+        here = tiles[:2] if last else tiles
+        shift(layer, 0)
         for k in range(3):
-            loads[3 * layer + k].wait()
-
-        @pl.loop(0, pieces)
-        def _(m, layer=layer, width=width):
-            own_part(layer, m, width)
-
-        for m in range(pieces):
-            copies[m].wait_recv()
-
-            @pl.loop(0, step // BLOCK)
-            def _(j, m=m, layer=layer):
-                rows = pl.ds(pl.multiple_of(m * step + j * BLOCK, BLOCK), BLOCK)
-                shifted(layer, 1, rows, u[layer, 1, rows, :].astype(jnp.float32))
-
-        for m in range(pieces):
-            copies[m].wait_send()
+            loads[6 * layer + k].wait()
+        for start, size in here:
+            acc[:, start : start + size] = dot(
+                w[layer, 0], u[layer, 0, :, start : start + size]
+            )
+        for cp in copies:
+            cp.wait()
+        shift(layer, 1)
+        for k in range(3):
+            loads[6 * layer + 3 + k].wait()
         copies = []
-        if last:
-
-            @pl.loop(0, pieces)
-            def _(m, layer=layer, width=width):
-                rows, val = other_part(layer, m, width)
-                x_out[rows, :] = val
-        else:
-            for m in range(pieces):
-                rows, val = other_part(layer, m, width)
-                xe[layer + 1, rows, :] = val
-                activate(layer + 1, m)
+        for m, (start, size) in enumerate(here):
+            lanes = slice(start, start + size)
+            t = acc[:, lanes] + dot(w[layer, 1], u[layer, 1, :, lanes])
+            val = (xe[layer, :, lanes].astype(jnp.float32) + t).astype(jnp.bfloat16)
+            if last:
+                x_out[:, lanes] = val
+            else:
+                xe[layer + 1, :, lanes] = val
+                activate(layer + 1, tiles[m])
                 cp = u_copy(layer + 1, m)
                 cp.start()
                 copies.append(cp)
@@ -335,10 +337,9 @@
         in_specs=[vmem] * 6 + [pl.BlockSpec(memory_space=pl.ANY)],
         out_specs=[vmem, vmem, vmem],
         scratch_shapes=[
-            pltpu.VMEM(w.shape, bf16),
+            pltpu.VMEM((LAYERS, 2, c, 3 * c), bf16),
             pltpu.VMEM((LAYERS, c, wide), bf16),
-            pltpu.VMEM((LAYERS, 2, c, wide), bf16),
-            pltpu.VMEM((LAYERS, 2, 2, c, wide), bf16),
+            pltpu.VMEM((LAYERS, 2, 3 * c, wide), bf16),
             pltpu.VMEM((c, wide), f32),
             pltpu.VMEM((2, EDGE, c), bf16),
             pltpu.VMEM((2, EDGE, c), bf16),
@@ -346,7 +347,7 @@
             pltpu.VMEM((LIST * BLOCK, n), bf16),
             pltpu.VMEM((LIST * BLOCK, n), bf16),
             pltpu.VMEM((LIST * BLOCK, n), bf16),
-            pltpu.SemaphoreType.DMA((LAYERS, 3)),
+            pltpu.SemaphoreType.DMA((LAYERS, 2, 3)),
             pltpu.SemaphoreType.DMA((2,)),
             pltpu.SemaphoreType.DMA((2,)),
             pltpu.SemaphoreType.DMA((LAYERS, 3)),

time: 105 us -> 103 us (0.981)
  Pallas kernels: 93.9 us -> 92.5 us
    pallas_call x1, Pallas kernels: 4.24 us -> 3.17 us  [pick(): pl.pallas_call(pick_kernel, grid_spec=pltpu.PrefetchScalarGridSpec(num_sc...]
where the time goes in v3:
time: 103 us
  Pallas kernels  92.5 us (90%)
  local copies, waits for them, and re-layouts  8.81 us (9%)
  between operations  1.36 us (1%)
    pallas_call x1, Pallas kernels, scatter(): pl.pallas_call(scatter_kernel, out_shape=jax.ShapeDtypeStruct((2 * BLOCK,...  45.2 us
    pallas_call x1, Pallas kernels, trunk(): pl.pallas_call(trunk_kernel, out_shape=[jax.ShapeDtypeStruct((c, n), bf16...  44.1 us
    unnamed x13, local copies, waits for them, and re-layouts  5.55 us
    pallas_call x1, Pallas kernels, pick(): pl.pallas_call(pick_kernel, grid_spec=pltpu.PrefetchScalarGridSpec(num_sc...  3.17 us

profile of v3, /device:TPU:0, one launch (start us, length us, event | category | flops | bytes accessed | tf_op | source)
XLA Modules:
  0.0 102.8 jit_solution(4240654201605257761)
XLA Ops:
  0.6 2.4 %copy.21 = bf16[128,8,4,128]{3,1,2,0:T(8,128)(2,1)} copy(bf16[128,8,4,128]{3,2,1,0:T(4,128)(2,1)} %bitcast.21) | data formatting | bytes 2097152
  3.0 0.0 copy-start.2
  3.0 0.0 copy-start.3
  3.0 0.0 copy-start.4
  3.0 3.2 %pick.1.hw = bf16[512,768]{1,0:T(8,128)(2,1)} custom-call(s32[4]{0:T(128)} %bitcast.25, bf16[768,4096]{1,0:T(8,128)(2,1)} %refs_3_.1, bf16[768,4096]{1,0:T(8,128)(2,1)} %refs_3_.1, bf16[768,4096]{1,0:T(8,128)(2,1)} %refs_3_.1, bf16[768,4096]{1,0:T(8,128)(2,1)} %refs_3_.1), custom_call_target="tpu_custom_call" | custom-call | tf_op jit(solution)/shard_map/pick/pallas_call | solution.py:104
  6.2 0.0 copy-done.2
  6.2 0.0 copy-done.3
  6.2 0.9 copy.17
  7.8 0.1 broadcast_in_dim.13
  7.9 0.9 copy.18.act
  8.7 0.0 copy-done.4
  8.8 0.6 pad.4.ids
  9.3 44.1 %trunk.1 = (bf16[768,1024]{1,0:T(8,128)(2,1)}, bf16[512,768]{1,0:T(8,128)(2,1)}, s32[3,8,128]{2,1,0:T(8,128)}) custom-call(bf16[768,1024]{1,0:T(8,128)(2,1)} %feat.1, f32[768,4]{1,0:T(8,128)} %bitcast.23, f32[512,1]{1,0:T(8,128)} %copy.18.act, s32[8,128]{1,0:T(8,128)} %pad.4.ids, bf16[512,768]{1,0:T(8,128)(2,1)} %pick.1.hw, bf16[1024,512]{1,0:T(8,128)(2,1)} %bitcast.22, ...), custom_call_target="tpu_custom_call" | custom-call | flops 16999999488 | bytes 20971520 | tf_op jit(solution)/shard_map/trunk/pallas_call | solution.py:330
  53.5 0.7 slice_bitcast_fusion.2
  54.3 0.1 select_reduce_fusion
  54.4 0.1 reshape.263.table
  54.5 0.0 copy-start
  54.5 1.1 %copy-done = bf16[512,768]{1,0:T(8,128)(2,1)S(1)} copy-done((bf16[512,768]{1,0:T(8,128)(2,1)S(1)}, bf16[512,768]{1,0:T(8,128)(2,1)}, u32[]{:S(2)}) %copy-start) | copy-done | bytes 786456
  55.6 0.0 copy-start.1
  55.6 45.2 %scatter.1 = f32[256,768]{1,0:T(8,128)S(1)} custom-call(s32[128]{0:T(128)S(1)} %reshape.263.table, bf16[512,768]{1,0:T(8,128)(2,1)S(1)} %copy-done), custom_call_target="tpu_custom_call" | custom-call | tf_op jit(solution)/shard_map/scatter/pallas_call | solution.py:481
  100.8 0.0 copy-done.1
  100.8 1.1 %copy.25 = bf16[768,1024]{1,0:T(8,128)(2,1)} copy(bf16[768,1024]{1,0:T(8,128)(2,1)S(1)} %copy-done.1) | data formatting | bytes 3145728
  102.0 0.9 copy.26
  (7 shorter events, 0.1 us)
Async XLA Ops:
  3.0 3.2 %copy-start.2 = (f32[2,768]{1,0:T(2,128)S(1)}, f32[2,768]{1,0:T(2,128)}, u32[]{:S(2)}) copy-start(f32[2,768]{1,0:T(2,128)} %param.10) | copy-start | bytes 18436
  3.0 3.2 %copy-start.3 = (f32[2,768]{1,0:T(2,128)S(1)}, f32[2,768]{1,0:T(2,128)}, u32[]{:S(2)}) copy-start(f32[2,768]{1,0:T(2,128)} %param.9) | copy-start | bytes 18436
  3.0 5.7 %copy-start.4 = (s32[1,4]{1,0:T(1,128)S(1)}, s32[1,4]{1,0:T(1,128)}, u32[]{:S(2)}) copy-start(s32[1,4]{1,0:T(1,128)} %param.13) | copy-start | bytes 52
  54.5 1.1 %copy-start = (bf16[512,768]{1,0:T(8,128)(2,1)S(1)}, bf16[512,768]{1,0:T(8,128)(2,1)}, u32[]{:S(2)}) copy-start(bf16[512,768]{1,0:T(8,128)(2,1)} %get-tuple-element.7.term) | copy-start | bytes 2359300
  55.6 45.2 %copy-start.1 = (bf16[768,1024]{1,0:T(8,128)(2,1)S(1)}, bf16[768,1024]{1,0:T(8,128)(2,1)}, u32[]{:S(2)}) copy-start(bf16[768,1024]{1,0:T(8,128)(2,1)} %get-tuple-element.20) | copy-start | bytes 4718596
